TPU v7x, 32 devices: a whole 2x2x4 slice. The times are simulated.
32 devices in a mesh: trace: 4 (over x, core), seq: 8 (over z, y).
Axes of the slice: x: 2, y: 2, z: 4, core: 2. Of those that a mesh axis runs over, the one named last changes fastest.
Arguments:
- tokens: bfloat16 [32768, 1024], P(('trace', 'seq')), parts along dimension 0, may hold values from -6 to 6
- norm_gain: float32 [1024], replicated, may hold values from 0.1 to 1.9
- w_qkv: bfloat16 [1024, 3072], replicated, may hold values from -0.02734375 to 0.02734375
- conv_weight: float32 [4, 3072], replicated, may hold values from -3 to 3
- head_gain: float32 [1024], replicated, may hold values from 0.1 to 1.9
- w_out: bfloat16 [1024, 1024], replicated, may hold values from -0.1875 to 0.1875
Outputs:
- layer_out: bfloat16 [32768, 1024], P(('trace', 'seq')), parts along dimension 0
There are 4 independent parts, one for each index of `trace`. A program takes and returns all parts, laid end to end along the dimension named above; an argument that names none is the same for every part. Nothing has to cross between parts.
All inputs are finite; a program needn't handle non-finite values.
Results may differ from a plain program's by a relative error of at most 0.012.
Values may be sent and summed in bfloat16 or wider, within the bound.
A program may use at most 128 MiB of HBM per device.

v0:
```python
import jax
import jax.numpy as jnp
from jax import lax
from jax.sharding import PartitionSpec as P

H = 8
DH = 128
KW = 4


def from_behind(value, axis, steps):
    count = lax.axis_size(axis)
    first, last = (max(0, -steps), min(count, count - steps))
    return lax.ppermute(value, axis, [(source, source + steps) for source in range(first, last)])


def entering(x, axis, join, neutral):
    place = lax.axis_index(axis)
    gathered = lax.all_gather(x.astype(jnp.bfloat16), axis)
    state = jnp.zeros_like(x) + jnp.asarray(neutral, x.dtype)

    def one(hop, state):
        return join(state, lax.dynamic_index_in_dim(gathered, hop, 0, False).astype(x.dtype))

    return lax.fori_loop(0, place, one, state)


def input_norm(values, norm_gain):
    values_f = values.astype(jnp.float32)
    scale = lax.rsqrt(jnp.mean(values_f * values_f, -1, keepdims=True) + 1e-06)
    return (values_f * scale * norm_gain).astype(jnp.bfloat16)


def add_states(earlier, later):
    return earlier + later


def local(tokens, norm_gain, w_qkv, conv_weight, head_gain, w_out):
    row_count = tokens.shape[0]
    model_width = tokens.shape[1]
    normed = input_norm(tokens, norm_gain)
    projected = jnp.dot(normed, w_qkv, preferred_element_type=jnp.float32).astype(jnp.bfloat16)
    earlier_rows = from_behind(projected[row_count - (KW - 1) :], "seq", 1)
    padded = jnp.concatenate([earlier_rows, projected], 0)
    summed = jnp.zeros(projected.shape, jnp.float32)
    for offset in range(KW):
        begin = KW - 1 - offset
        summed = summed + conv_weight[offset] * padded[begin : begin + row_count].astype(
            jnp.float32
        )
    mixed = jax.nn.silu(summed).astype(jnp.bfloat16)
    block_rows = min(512, row_count)
    count = row_count // block_rows
    query_rows = mixed[:, :model_width].reshape(count, block_rows, H, DH)
    key_rows = mixed[:, model_width : 2 * model_width].reshape(count, block_rows, H, DH)
    value_rows = mixed[:, 2 * model_width :].reshape(count, block_rows, H, DH)
    block_states = jnp.einsum(
        "bthd,bthe->bhde", key_rows, value_rows, preferred_element_type=jnp.float32
    )
    local_state = jnp.sum(block_states, 0)
    empty_state = jnp.zeros((H, DH, DH), jnp.float32)
    prefix = entering(local_state, "seq", add_states, empty_state)
    causal = jnp.tril(jnp.ones((block_rows, block_rows), jnp.bool_))

    def advance(carried, blocks):
        query_block, key_block, value_block, block_state = blocks
        carried_part = jnp.einsum(
            "thd,hde->the",
            query_block.astype(jnp.float32),
            carried,
            precision=lax.Precision.HIGHEST,
        )
        scores = jnp.einsum(
            "thd,shd->hts", query_block, key_block, preferred_element_type=jnp.float32
        )
        scores = jnp.where(causal[None], scores, 0.0).astype(jnp.bfloat16)
        local_part = jnp.einsum(
            "hts,she->the", scores, value_block, preferred_element_type=jnp.float32
        )
        return (carried + block_state, carried_part + local_part)

    _, attended = lax.scan(advance, prefix, (query_rows, key_rows, value_rows, block_states))
    attended = attended.reshape(row_count, H, DH)
    scaled = attended * lax.rsqrt(jnp.mean(attended * attended, -1, keepdims=True) + 1e-05)
    headed = (scaled.reshape(row_count, model_width) * head_gain).astype(jnp.bfloat16)
    return jnp.dot(headed, w_out, preferred_element_type=jnp.float32).astype(jnp.bfloat16)


def solution(mesh):
    placed = (P(("trace", "seq"), None), P(), P(), P(), P(), P())
    return jax.shard_map(
        local, mesh=mesh, in_specs=placed, out_specs=P(("trace", "seq"), None), check_vma=False
    )
```

profile of v0, /device:TPU:28, one launch (start us, length us, event | category | flops | bytes accessed | tf_op | source)
XLA Modules:
  0.0 154.0 jit_solution(764234529074062347)
XLA Ops:
  6.5 0.0 copy-start
  6.5 0.0 all-gather.3.cloned.1.call-start
  6.5 2.2 %fusion.12 = f32[1024]{0:T(1024)S(1)} fusion(bf16[1024,1024]{1,0:T(8,128)(2,1)} %param.10), kind=kLoop, calls=%fused_computation.28 | loop fusion | flops 3144704 | bytes 2101248 | tf_op jit(solution)/shard_map/reduce_sum | solution.py:30
  8.8 0.0 copy-start.6
  8.8 9.6 %convolution_convert_fusion = bf16[1024,3072]{1,0:T(8,128)(2,1)S(1)} fusion(bf16[1024,3072]{1,0:T(8,128)(2,1)} %param.12, bf16[1024,1024]{1,0:T(8,128)(2,1)} %param.10, f32[1024]{0:T(1024)} %param.11, f32[1024]{0:T(1024)S(1)} %add_rsqrt_fusion.1), kind=kOutput, calls=%fused_computation.25 | convolution fusion | flops 6449790976 | bytes 14688256 | tf_op jit(solution)/shard_map/dot_general | solution.py:42
  18.4 1.3 collective-permute-start
  19.7 0.0 copy-done.6
  19.7 4.4 %collective-permute-done = bf16[3,3072]{1,0:T(4,128)(2,1)S(1)} collective-permute-done((bf16[3,3072]{1,0:T(4,128)(2,1)S(1)}, bf16[3,3072]{1,0:T(4,128)(2,1)S(1)}, u32[]{:S(2)}, u32[]{:S(2)}) %collective-permute-start) | collective-permute-done | bytes 18464 | tf_op jit(solution)/shard_map/ppermute | solution.py:14
  24.1 8.6 %multiply_convert_fusion = bf16[1024,3072]{1,0:T(8,128)(2,1)S(1)} fusion(bf16[1024,3072]{1,0:T(8,128)(2,1)S(1)} %convolution_convert_fusion, bf16[3,3072]{1,0:T(4,128)(2,1)S(1)} %collective-permute-done, f32[3072]{0:T(1024)S(1)} %bitcast.94, f32[3072]{0:T(1024)S(1)} %bitcast.95, f32[3072]{0:T(1024)S(1)} %bitcast.93, f32[3072]{0:T(1024)S(1)} %bitcast.92), kind=kLoop, calls=%fused_computation.19 | loop fusion | flops 78643200 | bytes 12650496 | tf_op jit(solution)/shard_map/convert_element_type | solution.py:51
  32.7 3.5 %slice_bitcast_fusion = (bf16[128,8,8,128]{3,1,2,0:T(8,128)(2,1)}, bf16[128,8,8,128]{3,1,2,0:T(8,128)(2,1)S(1)}, bf16[128,8,8,128]{3,1,2,0:T(8,128)(2,1)S(1)}) fusion(bf16[1024,3072]{1,0:T(8,128)(2,1)S(1)} %multiply_convert_fusion), kind=kLoop, calls=%fused_computation.36 | loop fusion | bytes 12582912
  36.3 0.6 copy.37
  36.9 0.6 copy.38
  37.5 1.4 copy-done.3
  38.9 2.9 %fusion.30 = (bf16[8,128,128]{2,1,0:T(8,128)(2,1)}, f32[2,8,128,128]{3,2,1,0:T(8,128)}) fusion(bf16[2,512,8,128]{3,2,1,0:T(8,128)(2,1)S(1)} %bitcast.85, bf16[2,512,8,128]{3,2,1,0:T(8,128)(2,1)S(1)} %bitcast.83), kind=kOutput, calls=%fused_computation.49 | convolution fusion | flops 268566528 | bytes 5505024 | tf_op jit(solution)/shard_map/bthd,bthe->bhde/dot_general | solution.py:57
  41.8 0.0 all-gather.3.cloned.1.call-update
  41.9 3.6 %copy.39 = bf16[128,8,8,128]{3,2,1,0:T(8,128)(2,1)} copy(bf16[128,8,8,128]{3,1,2,0:T(8,128)(2,1)} %get-tuple-element.140) | data formatting | bytes 4194304
  45.4 44.3 %all-gather.3.cloned.1.call-done = bf16[64,128,128]{2,1,0:T(8,128)(2,1)} async-done(((bf16[8,128,128]{2,1,0:T(8,128)(2,1)}), bf16[64,128,128]{2,1,0:T(8,128)(2,1)}) %all-gather.3.cloned.1.call-update) | async-done | bytes 2097168 | tf_op jit(solution)/shard_map/all_gather | solution.py:19
  89.8 7.9 %while.23 = (s32[]{:T(128)}, f32[8,128,128]{2,1,0:T(8,128)S(1)}, s32[]{:T(128)}, bf16[8,8,128,128]{3,2,1,0:T(8,128)(2,1)}, s32[]{:T(128)}, /*index=5*/s32[]{:T(128)}, s32[]{:T(128)}) while((s32[]{:T(128)}, f32[8,128,128]{2,1,0:T(8,128)S(1)}, s32[]{:T(128)}, bf16[8,8,128,128]{3,2,1,0:T(8,128)(2,1)}, s32[]{:T(128)}, /*index=5*/s32[]{:T(128)}, ...), condition=%wide.region_3.4_spmd, body=%wide.region_2.3_spmd.sunk | while | flops 262149 | bytes 1310835 | solution.py:25
  89.8 1.1 convert_add_fusion.2
  90.9 1.1 convert_add_fusion.2
  92.0 1.1 convert_add_fusion.2
  93.1 1.1 convert_add_fusion.2
  94.2 1.1 convert_add_fusion.2
  95.3 1.1 convert_add_fusion.2
  96.4 1.1 convert_add_fusion.2
  97.7 35.1 %while.24 = (s32[]{:T(128)}, f32[8,128,128]{2,1,0:T(8,128)S(1)}, f32[2,512,8,128]{3,1,2,0:T(8,128)}, f32[2,8,128,128]{3,2,1,0:T(8,128)}, bf16[2,512,8,128]{3,2,1...) while((s32[]{:T(128)}, f32[8,128,128]{2,1,0:T(8,128)S(1)}, ...), condition=%wide.region_5.6_spmd.clone, body=%wide.region_4.5_spmd.clone.sunk | while | flops 1884160000 | bytes 25690748 | solution.py:82
  97.7 3.0 %constant_dynamic-slice_fusion.6 = (bf16[1,512,8,128]{3,2,1,0:T(8,128)(2,1)}, bf16[1,512,8,128]{3,2,1,0:T(8,128)(2,1)}) fusion(bf16[2,512,8,128]{3,2,1,0:T(8,128)(2,1)} %get-tuple-element.265, s32[]{:T(128)} %get-tuple-element.251, bf16[2,512,8,128]{3,2,1,0:T(8,128)(2,1)} %get-tuple-element.264), kind=kLoop, calls=%fused_computation.15.clone.1 | loop fusion | bytes 4194308 | tf_op jit(solution)/shard_map/while/body/jit(dynamic_index_in_dim)/dynamic_slice | solution.py:82
  100.7 2.4 %copy.72 = bf16[1,512,8,128]{1,3,2,0:T(8,128)(2,1)} copy(bf16[1,512,8,128]{3,2,1,0:T(8,128)(2,1)} %get-tuple-element.221) | data formatting | bytes 2097152 | tf_op jit(solution)/shard_map/while/body/jit(dynamic_index_in_dim)/dynamic_slice | solution.py:82
  103.1 1.3 constant_dynamic-slice_fusion.5
  104.5 1.0 copy-done.1
  105.4 2.3 %fusion.39 = f32[8,512,128]{2,1,0:T(8,128)} fusion(f32[8,128,128]{2,1,0:T(8,128)S(1)} %get-tuple-element.252, bf16[1,512,8,128]{3,2,1,0:T(8,128)(2,1)S(1)} %constant_dynamic-slice_fusion.5), kind=kOutput, calls=%fused_computation.13.clone.1 | convolution fusion | flops 805306368 | bytes 3670016 | tf_op jit(solution)/shard_map/while/body/eval_jaxpr/thd,hde->the/dot_general | solution.py:67
  107.7 0.1 iota_compare_fusion.2
  107.8 6.3 %bitcast_dynamic-update-slice_fusion.2 = f32[2,512,8,128]{3,1,2,0:T(8,128)} fusion(f32[2,512,8,128]{3,1,2,0:T(8,128)} %get-tuple-element.253, s32[]{:T(128)} %get-tuple-element.251, f32[8,512,128]{2,1,0:T(8,128)} %fusion.39, pred[512,512]{1,0:T(8,128)(4,1)S(1)} %iota_compare_fusion.2, bf16[1,512,8,128]{3,2,1,0:T(8,128)(2,1)} %get-tuple-element.220, ...), kind=kOutput, calls=%fused_computation.7.clone.1 | convolution fusion | flops 1078460416 | bytes 7602688 | tf_op jit(solution)/shard_map/while/body/eval_jaxpr/hts,she->the/dot_general | solution.py:77
  114.1 1.2 bitcast_add_fusion.3
  115.3 3.0 %constant_dynamic-slice_fusion.6 = (bf16[1,512,8,128]{3,2,1,0:T(8,128)(2,1)}, bf16[1,512,8,128]{3,2,1,0:T(8,128)(2,1)}) fusion(bf16[2,512,8,128]{3,2,1,0:T(8,128)(2,1)} %get-tuple-element.265, s32[]{:T(128)} %get-tuple-element.251, bf16[2,512,8,128]{3,2,1,0:T(8,128)(2,1)} %get-tuple-element.264), kind=kLoop, calls=%fused_computation.15.clone.1 | loop fusion | bytes 4194308 | tf_op jit(solution)/shard_map/while/body/jit(dynamic_index_in_dim)/dynamic_slice | solution.py:82
  118.3 2.4 %copy.72 = bf16[1,512,8,128]{1,3,2,0:T(8,128)(2,1)} copy(bf16[1,512,8,128]{3,2,1,0:T(8,128)(2,1)} %get-tuple-element.221) | data formatting | bytes 2097152 | tf_op jit(solution)/shard_map/while/body/jit(dynamic_index_in_dim)/dynamic_slice | solution.py:82
  120.7 1.3 constant_dynamic-slice_fusion.5
  122.0 1.0 copy-done.1
  123.0 2.3 %fusion.39 = f32[8,512,128]{2,1,0:T(8,128)} fusion(f32[8,128,128]{2,1,0:T(8,128)S(1)} %get-tuple-element.252, bf16[1,512,8,128]{3,2,1,0:T(8,128)(2,1)S(1)} %constant_dynamic-slice_fusion.5), kind=kOutput, calls=%fused_computation.13.clone.1 | convolution fusion | flops 805306368 | bytes 3670016 | tf_op jit(solution)/shard_map/while/body/eval_jaxpr/thd,hde->the/dot_general | solution.py:67
  125.3 0.1 iota_compare_fusion.2
  125.4 6.2 %bitcast_dynamic-update-slice_fusion.2 = f32[2,512,8,128]{3,1,2,0:T(8,128)} fusion(f32[2,512,8,128]{3,1,2,0:T(8,128)} %get-tuple-element.253, s32[]{:T(128)} %get-tuple-element.251, f32[8,512,128]{2,1,0:T(8,128)} %fusion.39, pred[512,512]{1,0:T(8,128)(4,1)S(1)} %iota_compare_fusion.2, bf16[1,512,8,128]{3,2,1,0:T(8,128)(2,1)} %get-tuple-element.220, ...), kind=kOutput, calls=%fused_computation.7.clone.1 | convolution fusion | flops 1078460416 | bytes 7602688 | tf_op jit(solution)/shard_map/while/body/eval_jaxpr/hts,she->the/dot_general | solution.py:77
  131.6 1.2 bitcast_add_fusion.3
  132.8 3.5 %multiply_reduce_fusion = f32[2,512,8]{1,2,0:T(8,128)S(1)} fusion(f32[2,512,8,128]{3,1,2,0:T(8,128)} %get-tuple-element.71), kind=kLoop, calls=%fused_computation.34 | loop fusion | flops 2088960 | bytes 4227072 | tf_op jit(solution)/shard_map/reduce_sum | solution.py:84
  136.3 4.4 %copy.31 = f32[2,512,8,128]{3,2,1,0:T(8,128)} copy(f32[2,512,8,128]{3,1,2,0:T(8,128)S(1)} %copy-done.4) | data formatting | bytes 8388608 | tf_op jit(solution)/shard_map/while | solution.py:82
  140.7 0.2 copy.32
  140.9 1.1 mul.105
  142.1 1.0 copy-done.5
  143.1 4.1 %fusion.26 = bf16[1024,1024]{1,0:T(8,128)(2,1)} fusion(bf16[1024,1024]{1,0:T(8,128)(2,1)S(1)} %copy-done, f32[128,8,8,128]{3,2,1,0:T(8,128)S(1)} %bitcast.88, f32[128,8,8,128]{3,2,1,0:T(8,128)S(1)} %bitcast.89, f32[1024]{0:T(1024)S(1)} %copy-done.7), kind=kOutput, calls=%fused_computation.45 | convolution fusion | flops 2151677952 | bytes 12587008 | tf_op jit(solution)/shard_map/dot_general | solution.py:86
  (17 shorter events, 0.1 us)
Async XLA Ops:
  6.5 135.5 %copy-start = (bf16[1024,1024]{1,0:T(8,128)(2,1)S(1)}, bf16[1024,1024]{1,0:T(8,128)(2,1)}, u32[]{:S(2)}) copy-start(bf16[1024,1024]{1,0:T(8,128)(2,1)} %param.15) | copy-start | bytes 6291460
  6.5 83.2 %all-gather.3.cloned.1.call-start = ((), (), s32[]{:S(2)}) async-start(), calls=%async_computation | async-start | bytes 2359296 | tf_op jit(solution)/shard_map/all_gather | solution.py:19
  8.8 10.9 %copy-start.6 = (f32[4,3072]{1,0:T(4,128)S(1)}, f32[4,3072]{1,0:T(4,128)}, u32[]{:S(2)}) copy-start(f32[4,3072]{1,0:T(4,128)} %param.13) | copy-start | bytes 147460
  18.4 5.7 %collective-permute-start = (bf16[3,3072]{1,0:T(4,128)(2,1)S(1)}, bf16[3,3072]{1,0:T(4,128)(2,1)S(1)}, u32[]{:S(2)}, u32[]{:S(2)}) collective-permute-start(bf16[3,3072]{1,0:T(4,128)(2,1)S(1)} %slice.44), channel_id=1, source_target_pairs={{0,1},{1,2},{2,3},{3,4},{4,5},{5,6},{6,7},{8,9},{9,10},{10,11},{11... | collective-permute-start | bytes 55304 | tf_op jit(solution)/shard_map/ppermute | solution.py:14
  36.9 4.9 %copy-start.2 = (bf16[128,8,8,128]{3,2,1,0:T(8,128)(2,1)}, bf16[128,8,8,128]{3,2,1,0:T(8,128)(2,1)S(1)}, u32[]{:S(2)}) copy-start(bf16[128,8,8,128]{3,2,1,0:T(8,128)(2,1)S(1)} %copy.37) | copy-start | bytes 6291460
  37.5 1.4 copy-start.3
  104.4 1.0 copy-start.1
  122.0 1.0 copy-start.1
  132.8 3.5 %copy-start.4 = (f32[2,512,8,128]{3,1,2,0:T(8,128)S(1)}, f32[2,512,8,128]{3,1,2,0:T(8,128)}, u32[]{:S(2)}) copy-start(f32[2,512,8,128]{3,1,2,0:T(8,128)} %get-tuple-element.71) | copy-start | bytes 12582916
  140.7 1.4 copy-start.7
  140.9 2.2 %copy-start.5 = (f32[2,512,8,128]{3,2,1,0:T(8,128)S(1)}, f32[2,512,8,128]{3,2,1,0:T(8,128)}, u32[]{:S(2)}) copy-start(f32[2,512,8,128]{3,2,1,0:T(8,128)} %copy.31) | copy-start | bytes 12582916
Sparse Core Ops, SparseCore 0:
  42.0 47.7 all-gather.2
where the time goes:
time: 155 us; the launch traced here: 154 us
  waiting for transfers between devices  48.7 us (31%)
  matrix products  33.7 us (22%)
  local copies, waits for them, and re-layouts  32 us (21%)
  other arithmetic  24.3 us (16%)
  between operations  13.6 us (9%)
    all_gather x1, waiting for transfers between devices, entering(): gathered = lax.all_gather(x.astype(jnp.bfloat16), axis)  44.3 us
    dynamic_slice x6, local copies, waits for them, and re-layouts, local(): lax.scan(advance, prefix, (query_rows, key_rows, value_rows, block_states))  13.5 us
    dot_general x2, matrix products, advance(): jnp.einsum('hts,she->the', scores, value_block, preferred_element_type=jn...  12.5 us
    unnamed x18, local copies, waits for them, and re-layouts  10.7 us
    dot_general x1, matrix products, local(): jnp.dot(normed, w_qkv, preferred_element_type=jnp.float32)  9.55 us
    convert_element_type x1, other arithmetic, local(): mixed = jax.nn.silu(summed).astype(jnp.bfloat16)  8.64 us
    add x7, other arithmetic, add_states(): return earlier + later  7.49 us
    dot_general x2, matrix products, advance(): jnp.einsum('thd,hde->the', query_block.astype(jnp.float32), carried, prec...  4.6 us
  transfers between devices with their start and end apart: 2, of which 2 were waited for; matrix products, arithmetic and copies ran while one was open for 2% of the time, Pallas kernels for 0%

commit v1 on v0

v1 whole, which is shorter than its diff:
```python
import functools

import jax
import jax.numpy as jnp
from jax import lax
from jax.experimental import pallas as pl
from jax.experimental.pallas import tpu as pltpu
from jax.sharding import PartitionSpec as P

H = 8
DH = 128
KW = 4
PW = 2 * DH
PAIRS = H // 2
HALO = 16
BLK = 256
SUB = 64
SKEW = 2

bf16 = jnp.bfloat16
f32 = jnp.float32


def kernel(
    n_seq, rows,
    tok_hbm, ng_hbm, w_hbm, cw_hbm, hg_hbm, wo_hbm, out_hbm,
    tok, halo, xn, ng, cw, hg, w, wo, pf, qs, ks, vs, att, hd, ost, cst, bd,
    ysend, yrecv, zsend, zrecv,
    tok_sem, w_sem, small_sem, wo_sem, out_sem,
    halo_ssem, halo_rsem, y_ssem, y_rsem, z_ssem, z_rsem,
):
    d_model = tok.shape[1]
    nblk = rows // BLK
    me = lax.axis_index("seq")
    odd = lax.rem(me, 2)
    place = me // 2
    depth = n_seq // 2
    partner = me + 1 - 2 * odd

    tok_rows = rows // 4
    def tok_copy(i):
        r = pl.ds(i * tok_rows, tok_rows)
        return pltpu.make_async_copy(tok_hbm.at[r], tok.at[r], tok_sem.at[i])
    def w_copy(c):
        return pltpu.make_async_copy(w_hbm.at[:, pl.ds(pl.multiple_of(c * PW, PW), PW)], w.at[c], w_sem.at[c])
    def wo_copy(c):
        return pltpu.make_async_copy(wo_hbm.at[:, pl.ds(pl.multiple_of(c * PW, PW), PW)], wo.at[c], wo_sem.at[c])
    def small_copies():
        return [
            pltpu.make_async_copy(ng_hbm, ng, small_sem.at[0]),
            pltpu.make_async_copy(cw_hbm, cw, small_sem.at[1]),
            pltpu.make_async_copy(hg_hbm, hg, small_sem.at[2]),
        ]

    barrier = pltpu.get_barrier_semaphore()
    for delta in (-2, -1, 1, 2):
        other = me + delta
        @pl.when((other >= 0) & (other < n_seq))
        def _():
            pl.semaphore_signal(
                barrier, inc=1, device_id={"seq": other}, device_id_type=pl.DeviceIdType.MESH
            )
    for c in small_copies():
        c.start()
    for i in range(4):
        tok_copy(i).start()
    for g in range(PAIRS):
        w_copy(PAIRS + g).start()
        w_copy(2 * PAIRS + g).start()
    for g in range(PAIRS):
        w_copy(g).start()
    for g in range(PAIRS):
        wo_copy(g).start()
    before = jnp.minimum(me, 2)
    after = jnp.minimum(n_seq - 1 - me, 2)
    pl.semaphore_wait(barrier, before + after)

    halo_copy = pltpu.make_async_remote_copy(
        src_ref=tok_hbm.at[pl.ds(rows - HALO, HALO)],
        dst_ref=halo,
        send_sem=halo_ssem,
        recv_sem=halo_rsem,
        device_id={"seq": me + 1},
        device_id_type=pl.DeviceIdType.MESH,
    )
    @pl.when(me < n_seq - 1)
    def _():
        halo_copy.start()
    @pl.when(me == 0)
    def _():
        halo[...] = jnp.zeros(halo.shape, bf16)
    @pl.when(place == 0)
    def _():
        zrecv[...] = jnp.zeros(zrecv.shape, bf16)
    bd[...] = jnp.zeros(bd.shape, bf16)

    def y_copy(g):
        return pltpu.make_async_remote_copy(
            src_ref=ysend.at[g], dst_ref=yrecv.at[g], send_sem=y_ssem.at[g], recv_sem=y_rsem.at[g],
            device_id={"seq": partner}, device_id_type=pl.DeviceIdType.MESH,
        )

    def z_copy(g):
        return pltpu.make_async_remote_copy(
            src_ref=zsend.at[g], dst_ref=zrecv.at[g], send_sem=z_ssem.at[g], recv_sem=z_rsem.at[g],
            device_id={"seq": me + 2}, device_id_type=pl.DeviceIdType.MESH,
        )

    def slot(p):
        g = p - SKEW * place

        @pl.when((g >= 0) & (g < PAIRS) & (place < depth - 1))
        def _():
            y_copy(g).wait_recv()

            @pl.when(place > 0)
            def _():
                z_copy(g).wait_recv()

            zsend[g] = (
                ysend[g].astype(f32) + yrecv[g].astype(f32) + zrecv[g].astype(f32)
            ).astype(bf16)
            z_copy(g).start()

    def norm(x, gain):
        xf = x.astype(f32)
        scale = lax.rsqrt(jnp.mean(xf * xf, -1, keepdims=True) + 1e-06)
        return (xf * scale * gain).astype(bf16)

    for c in small_copies():
        c.wait()
    step = 32
    for i in range(4):
        tok_copy(i).wait()

        @pl.loop(0, tok_rows // step)
        def _(t):
            at = pl.multiple_of(i * tok_rows + t * step, step)
            xn[pl.ds(pl.multiple_of(HALO + at, 16), step), :] = norm(tok[pl.ds(at, step), :], ng[...])
    @pl.when(me > 0)
    def _():
        halo_copy.wait_recv()
    xn[0:HALO, :] = norm(halo[...], ng[...])

    half = rows // 2

    def project(c, slot_pf, dst, g):
        taps = [
            [0.5 * cw[j : j + 1, pl.ds(pl.multiple_of(c * PW + h * DH, DH), DH)] for j in range(KW)]
            for h in range(2)
        ]
        for part in range(2):
            lo = 0 if part == 0 else HALO + half
            hi = HALO + half * (part + 1)
            p = jnp.dot(xn[lo:hi, :], w[c], preferred_element_type=f32)
            for h in range(2):
                pf[slot_pf, h, lo:hi, :] = p[:, h * DH : (h + 1) * DH]
            for h in range(2):
                for r in range(part * half, (part + 1) * half, SUB):
                    acc = taps[h][0] * pf[slot_pf, h, HALO + r : HALO + r + SUB, :]
                    for j in range(1, KW):
                        acc += taps[h][j] * pf[slot_pf, h, HALO + r - j : HALO + r - j + SUB, :]
                    dst[g, r : r + SUB, h * DH : (h + 1) * DH] = (acc + acc * jnp.tanh(acc)).astype(bf16)

    @pl.loop(0, PAIRS)
    def _(g):
        w_copy(PAIRS + g).wait()
        w_copy(2 * PAIRS + g).wait()
        project(PAIRS + g, 0, ks, g)
        project(2 * PAIRS + g, 1, vs, g)
        total = None
        for b in range(nblk):
            r = slice(b * BLK, (b + 1) * BLK)
            s = lax.dot_general(
                ks[g, r, :], vs[g, r, :], (((0,), (0,)), ((), ())), preferred_element_type=f32
            )
            s = [s[0:DH, 0:DH], s[DH:PW, DH:PW]]
            total = s if total is None else [total[0] + s[0], total[1] + s[1]]
            if b < nblk - 1:
                cst[g, b, 0] = total[0]
                cst[g, b, 1] = total[1]
        ysend[g, 0] = total[0].astype(bf16)
        ysend[g, 1] = total[1].astype(bf16)
        y_copy(g).start()
        slot(g - 1)

    causal = (
        lax.broadcasted_iota(jnp.int32, (BLK, BLK), 0)
        >= lax.broadcasted_iota(jnp.int32, (BLK, BLK), 1)
    )

    @pl.loop(0, PAIRS)
    def _(g):
        w_copy(g).wait()
        project(g, 0, qs, g)
        for h in range(2):
            c = slice(h * DH, (h + 1) * DH)
            for b in range(nblk):
                r = slice(b * BLK, (b + 1) * BLK)
                s = lax.dot_general(
                    qs[g, r, c], ks[g, r, c], (((1,), (1,)), ((), ())), preferred_element_type=f32
                )
                s = jnp.where(causal, s, 0.0).astype(bf16)
                att[g, r, c] = jnp.dot(s, vs[g, r, c], preferred_element_type=f32)
        slot(PAIRS - 1 + g)

    first_left = 2 * PAIRS - 1
    for p in range(first_left, PAIRS + SKEW * max(depth - 2, 0)):
        slot(p)

    oddf = odd.astype(f32)

    @pl.loop(0, PAIRS)
    def _(g):
        @pl.when(place == depth - 1)
        def _():
            y_copy(g).wait_recv()

            @pl.when(place > 0)
            def _():
                z_copy(g).wait_recv()

        cols = pl.multiple_of(g * PW, PW)
        for h in range(2):
            c = slice(h * DH, (h + 1) * DH)
            prefix = zrecv[g, h].astype(f32) + oddf * yrecv[g, h].astype(f32)
            for b in range(nblk):
                carried = prefix if b == 0 else prefix + cst[g, b - 1, h]
                bd[b, c, c] = carried.astype(bf16)
        for b in range(nblk):
            r = slice(b * BLK, (b + 1) * BLK)
            both = att[g, r, :] + jnp.dot(qs[g, r, :], bd[b], preferred_element_type=f32)
            for h in range(2):
                a = both[:, h * DH : (h + 1) * DH]
                at = pl.multiple_of(g * PW + h * DH, DH)
                scale = lax.rsqrt(jnp.mean(a * a, -1, keepdims=True) + 1e-05)
                hd[r, pl.ds(at, DH)] = (a * scale * hg[:, pl.ds(at, DH)]).astype(bf16)

    def out_copy(c):
        return pltpu.make_async_copy(
            ost.at[c], out_hbm.at[:, pl.ds(pl.multiple_of(c * PW, PW), PW)], out_sem.at[c]
        )

    @pl.loop(0, d_model // PW)
    def _(c):
        wo_copy(c).wait()
        ost[c] = jnp.dot(hd[...], wo[c], preferred_element_type=f32).astype(bf16)
        out_copy(c).start()

    @pl.when(me < n_seq - 1)
    def _():
        halo_copy.wait_send()
    for g in range(PAIRS):
        y_copy(g).wait_send()

        @pl.when(place < depth - 1)
        def _():
            z_copy(g).wait_send()
    for c in range(d_model // PW):
        out_copy(c).wait()


def local(n_seq, tokens, norm_gain, w_qkv, conv_weight, head_gain, w_out):
    rows, d_model = tokens.shape
    nblk = rows // BLK
    groups = 3 * PAIRS
    any_spec = pl.BlockSpec(memory_space=pl.ANY)
    dma = pltpu.SemaphoreType.DMA
    state = pltpu.VMEM((PAIRS, 2, DH, DH), bf16)
    flops = 2 * rows * d_model * (4 * d_model) + 2 * rows * d_model * (2 * BLK + 4 * DH)
    return pl.pallas_call(
        functools.partial(kernel, n_seq, rows),
        out_shape=jax.ShapeDtypeStruct((rows, d_model), bf16),
        in_specs=[any_spec] * 6,
        out_specs=any_spec,
        scratch_shapes=[
            pltpu.VMEM((rows, d_model), bf16),
            pltpu.VMEM((HALO, d_model), bf16),
            pltpu.VMEM((rows + HALO, d_model), bf16),
            pltpu.VMEM((1, d_model), f32),
            pltpu.VMEM((KW, 3 * d_model), f32),
            pltpu.VMEM((1, d_model), f32),
            pltpu.VMEM((groups, d_model, PW), bf16),
            pltpu.VMEM((PAIRS, d_model, PW), bf16),
            pltpu.VMEM((2, 2, rows + HALO, DH), f32),
            pltpu.VMEM((PAIRS, rows, PW), bf16),
            pltpu.VMEM((PAIRS, rows, PW), bf16),
            pltpu.VMEM((PAIRS, rows, PW), bf16),
            pltpu.VMEM((PAIRS, rows, PW), f32),
            pltpu.VMEM((rows, d_model), bf16),
            pltpu.VMEM((PAIRS, rows, PW), bf16),
            pltpu.VMEM((PAIRS, nblk, 2, DH, DH), f32),
            pltpu.VMEM((nblk, PW, PW), bf16),
            state, state, state, state,
            dma((4,)), dma((groups,)), dma((3,)), dma((PAIRS,)), dma((PAIRS,)),
            dma, dma, dma((PAIRS,)), dma((PAIRS,)), dma((PAIRS,)), dma((PAIRS,)),
        ],
        compiler_params=pltpu.CompilerParams(
            collective_id=0, has_side_effects=True, vmem_limit_bytes=52 * 1024 * 1024
        ),
        cost_estimate=pl.CostEstimate(flops=flops, bytes_accessed=12 << 20, transcendentals=rows * 3 * d_model),
    )(tokens, norm_gain.reshape(1, -1), w_qkv, conv_weight, head_gain.reshape(1, -1), w_out)


def solution(mesh):
    placed = (P(("trace", "seq"), None), P(), P(), P(), P(), P())
    return jax.shard_map(
        functools.partial(local, mesh.shape["seq"]),
        mesh=mesh,
        in_specs=placed,
        out_specs=P(("trace", "seq"), None),
        check_vma=False,
    )
```

time: 155 us -> 37.8 us (0.24)
  waiting for transfers between devices: 48.7 us -> 0 us
  matrix products: 33.7 us -> 0 us
  Pallas kernels: 0 us -> 32.2 us
  local copies, waits for them, and re-layouts: 32 us -> 5.25 us
  other arithmetic: 24.3 us -> 0 us
  between operations: 13.6 us -> 0.01 us
    all_gather x1 -> x0, waiting for transfers between devices: 44.3 us -> none  [entering(): gathered = lax.all_gather(x.astype(jnp.bfloat16), axis)]
    dot_general x7 -> x0, matrix products: 33.7 us -> none  [the longest x2 12.5 us: advance(): jnp.einsum('hts,she->the', scores, value_block, preferred_element_type=jn...]
    pallas_call x0 -> x1, Pallas kernels: none -> 32.2 us  [local(): pl.pallas_call(functools.partial(kernel, n_seq, rows), out_shape=jax.Shap...]
    dynamic_slice x6 -> x0, local copies, waits for them, and re-layouts: 13.5 us -> none  [local(): lax.scan(advance, prefix, (query_rows, key_rows, value_rows, block_states))]
    add x9 -> x0, other arithmetic: 9.81 us -> none  [the longest x7 7.49 us: add_states(): return earlier + later]
    convert_element_type x1 -> x0, other arithmetic: 8.64 us -> none  [local(): mixed = jax.nn.silu(summed).astype(jnp.bfloat16)]
    while x5 -> x0, local copies, waits for them, and re-layouts: 6.33 us -> none  [the longest x1 4.38 us: local(): lax.scan(advance, prefix, (query_rows, key_rows, value_rows, block_states))]
    reduce_sum x2 -> x0, other arithmetic: 5.71 us -> none  [the longest x1 3.49 us: local(): jnp.mean(attended * attended, -1, keepdims=True) + 1e-05]
  transfers between devices with their start and end apart: 2 -> 0, of which waited for: 2 -> 0; matrix products, arithmetic and copies ran while one was open for 2% -> 0% of each run, Pallas kernels for 0% -> 0%
where the time goes in v1:
time: 37.8 us; the launch traced here: 37.4 us
  Pallas kernels  32.2 us (85%)
  local copies, waits for them, and re-layouts  5.25 us (14%)
    pallas_call x1, Pallas kernels, local(): pl.pallas_call(functools.partial(kernel, n_seq, rows), out_shape=jax.Shap...  32.2 us
    unnamed x7, local copies, waits for them, and re-layouts  5.25 us

profile of v1, /device:TPU:28, one launch (start us, length us, event | category | flops | bytes accessed | tf_op | source)
XLA Modules:
  0.0 37.4 jit_solution(8980252323829123123)
XLA Ops:
  0.0 0.0 copy-start
  0.0 0.8 %copy-done = f32[4,3072]{1,0:T(4,128)S(1)} copy-done((f32[4,3072]{1,0:T(4,128)S(1)}, f32[4,3072]{1,0:T(4,128)}, u32[]{:S(2)}) %copy-start) | copy-done | bytes 49176
  0.8 0.0 copy-start.1
  0.8 0.7 %copy-done.1 = f32[1024]{0:T(1024)S(1)} copy-done((f32[1024]{0:T(1024)S(1)}, f32[1024]{0:T(1024)}, u32[]{:S(2)}) %copy-start.1) | copy-done | bytes 4120
  1.5 0.0 copy-start.2
  1.5 0.7 %copy-done.2 = f32[1024]{0:T(1024)S(1)} copy-done((f32[1024]{0:T(1024)S(1)}, f32[1024]{0:T(1024)}, u32[]{:S(2)}) %copy-start.2) | copy-done | bytes 4120
  2.2 32.2 %shard_map.64 = bf16[1024,1024]{1,0:T(8,128)(2,1)} custom-call(bf16[1024,1024]{1,0:T(8,128)(2,1)} %tok_hbm.1, f32[1,1024]{1,0:T(1,128)S(1)} %bitcast.2, bf16[1024,3072]{1,0:T(8,128)(2,1)} %w_hbm.1, f32[4,3072]{1,0:T(4,128)S(1)} %copy-done, f32[1,1024]{1,0:T(1,128)S(1)} %bitcast.3, bf16[1024,1024]{1,0:T(8,128)(2,1)} %wo_hbm.1), custom_call_target="tpu_custom_call" | custom-call | flops 10737418240 | bytes 12582912 | tf_op jit(solution)/shard_map/pallas_call | solution.py:271
  34.4 3.1 %copy.8 = bf16[1024,1024]{1,0:T(8,128)(2,1)} copy(bf16[1024,1024]{1,0:T(8,128)(2,1)} %shard_map.64) | data formatting | bytes 4194304
Async XLA Ops:
  0.0 0.8 %copy-start = (f32[4,3072]{1,0:T(4,128)S(1)}, f32[4,3072]{1,0:T(4,128)}, u32[]{:S(2)}) copy-start(f32[4,3072]{1,0:T(4,128)} %cw_hbm.1) | copy-start | bytes 147460
  0.8 0.7 %copy-start.1 = (f32[1024]{0:T(1024)S(1)}, f32[1024]{0:T(1024)}, u32[]{:S(2)}) copy-start(f32[1024]{0:T(1024)} %param.7) | copy-start | bytes 12292
  1.5 0.7 %copy-start.2 = (f32[1024]{0:T(1024)S(1)}, f32[1024]{0:T(1024)}, u32[]{:S(2)}) copy-start(f32[1024]{0:T(1024)} %param.10) | copy-start | bytes 12292
